TPU v7x, 32 devices: a whole 2x2x4 slice. The times are simulated.
32 devices in a mesh: grp: 2 (over x), cell: 16 (over z, y, core).
Axes of the slice: x: 2, y: 2, z: 4, core: 2. Of those that a mesh axis runs over, the one named last changes fastest.
Arguments:
- fields: bfloat16 [8192, 3, 8192], P(('grp', 'cell')), parts along dimension 0, may hold values from -6 to 6
- horiz: float32 [16384], P(('grp', 'cell')), parts along dimension 0, may hold values from 0.2 to 1
- vertical: float32 [16384], P(('grp', 'cell')), parts along dimension 0, may hold values from 1.5 to 6
- tilt_angle: float32 [16384], P(('grp', 'cell')), parts along dimension 0, may hold values from 0.2 to 1.4
- azimuth: float32 [16384], P(('grp', 'cell')), parts along dimension 0, may hold values from -3.140625 to 3.140625
- electrode_quads: int32 [4096, 4], P('grp'), parts along dimension 0, may hold values from 0 to 4095, as said below
Outputs:
- jacobian: bfloat16 [4096, 4, 8192], P('grp', None, 'cell'), parts along dimension 0
- coverage: float32 [16384], P(('grp', 'cell')), parts along dimension 0
There are 2 independent parts, one for each index of `grp`. A program takes and returns all parts, laid end to end along the dimension named above; each array names one. Nothing has to cross between parts.
Inputs may be any that keep to these rules, and one draw needn't show every extreme that they name: `electrode_quads`: each row names four different electrodes.
All inputs are finite; a program needn't handle non-finite values.
Results may differ from a plain program's by a relative error of at most 0.001.
Values may be sent and summed in bfloat16 or wider, within the bound.
A program may use at most 192 MiB of HBM per device.

v0:
```python
import functools

import jax
import jax.numpy as jnp
from jax import lax
from jax.experimental import pallas as pl
from jax.experimental.pallas import tpu as pltpu
from jax.sharding import PartitionSpec as P

MESH = pl.DeviceIdType.MESH
LANES = 128


def greet(n, me):
    barrier = pltpu.get_barrier_semaphore()

    @pl.loop(1, n)
    def _(step):
        pl.semaphore_signal(barrier, inc=1, device_id={"cell": lax.rem(me + step, n)}, device_id_type=MESH)

    pl.semaphore_wait(barrier, n - 1)


def fill_coefficients(coef, horiz, vertical, sin_t, cos_t, sin_p, cos_p):
    axis = (sin_t * cos_p, sin_t * sin_p, cos_t)
    tilt = (cos_t * cos_p, cos_t * sin_p, -sin_t)
    turn = (-sin_t * sin_p, sin_t * cos_p, jnp.zeros_like(sin_t))
    contrast = vertical - horiz
    pairs = ((0, 0), (1, 1), (2, 2), (0, 1), (0, 2), (1, 2))
    rows = [-horiz * ((1.0 if i == j else 0.0) - axis[i] * axis[j]) for i, j in pairs]
    rows += [-vertical * axis[i] * axis[j] for i, j in pairs]
    for other in (tilt, turn):
        rows += [-contrast * (other[i] * axis[j] + axis[i] * other[j]) for i, j in pairs]
    for k, row in enumerate(rows):
        coef[k] = row


def chunk_sensitivities(chunk, quads, grads, coef, sens, squares, wide, diffs):
    comps, electrodes, _ = wide.shape
    readings = squares.shape[0]
    block = 256

    @pl.loop(0, electrodes // block)
    def _(i):
        at = pl.multiple_of(i * block, block)
        for c in range(comps):
            wide[c, pl.ds(at, block), :] = grads[c, pl.ds(at, block), :].astype(jnp.float32)

    @pl.loop(0, readings // 8)
    def _(g):
        at = pl.multiple_of(g * 8, 8)
        rows = []
        for u in range(8):
            a, b, m, n = (quads[j, at + u] for j in range(4))
            rows += [wide[c, pl.ds(a, 1), :] - wide[c, pl.ds(b, 1), :] for c in range(comps)]
            rows += [wide[c, pl.ds(m, 1), :] - wide[c, pl.ds(n, 1), :] for c in range(comps)]
        for u in range(8):
            for c in range(2 * comps):
                diffs[c, pl.ds(at + u, 1), :] = rows[2 * comps * u + c]

    tile = 16

    @pl.loop(0, readings // tile)
    def _(i):
        at = pl.multiple_of(i * tile, tile)
        s = [diffs[c, pl.ds(at, tile), :] for c in range(3)]
        r = [diffs[3 + c, pl.ds(at, tile), :] for c in range(3)]
        terms = [s[c] * r[c] for c in range(3)]
        terms += [s[i] * r[j] + s[j] * r[i] for i, j in ((0, 1), (0, 2), (1, 2))]
        square = squares[pl.ds(at, tile), :]
        for p in range(4):
            value = terms[0] * coef[6 * p, pl.ds(chunk, 1), :]
            for k in range(1, 6):
                value = value + terms[k] * coef[6 * p + k, pl.ds(chunk, 1), :]
            sens[pl.ds(4 * at + p, tile, stride=4), :] = value
            square = square + value * value
        squares[pl.ds(at, tile), :] = square


def exchange_kernel(
    n, quads, fields, horiz, vertical, sin_t, cos_t, sin_p, cos_p, sens, total,
    landed, ready, wide, diffs, squares, coef, part, slots,
    send_sem, recv_sem, own_sem, out_sem, part_send_sem, part_recv_sem,
):
    me = lax.axis_index("cell")
    rows = fields.shape[1]
    chunks = landed.shape[0]
    cells = chunks * LANES
    greet(n, me)

    def landing(chunk):
        return landed.at[chunk, :, pl.ds(pl.multiple_of(me * rows, rows), rows), :]

    def leaving(device, chunk):
        return fields.at[:, :, pl.ds(pl.multiple_of(device * cells + chunk * LANES, LANES), LANES)]

    def copy(chunk, step):
        peer = lax.rem(me + step, n)
        return pltpu.make_async_remote_copy(
            src_ref=leaving(peer, chunk),
            dst_ref=landing(chunk),
            send_sem=send_sem.at[chunk, step],
            recv_sem=recv_sem.at[chunk, step],
            device_id={"cell": peer},
            device_id_type=MESH,
        )

    def own(chunk):
        return pltpu.make_async_copy(leaving(me, chunk), landing(chunk), own_sem.at[chunk])

    def out(chunk):
        at = pl.ds(pl.multiple_of(chunk * LANES, LANES), LANES)
        return pltpu.make_async_copy(ready.at[chunk], sens.at[:, at], out_sem.at[chunk])

    @pl.loop(0, chunks)
    def _(chunk):
        own(chunk).start()

        @pl.loop(1, n)
        def _(step):
            copy(chunk, step).start()

    squares[...] = jnp.zeros_like(squares)
    fill_coefficients(coef, *(x[...] for x in (horiz, vertical, sin_t, cos_t, sin_p, cos_p)))

    @pl.loop(0, chunks)
    def _(chunk):
        own(chunk).wait()

        @pl.loop(1, n)
        def _(step):
            copy(chunk, step).wait()

        chunk_sensitivities(
            chunk, quads, landed.at[chunk], coef, ready.at[chunk], squares, wide, diffs
        )
        out(chunk).start()

    def copy_part(step):
        return pltpu.make_async_remote_copy(
            src_ref=part,
            dst_ref=slots.at[step],
            send_sem=part_send_sem.at[step],
            recv_sem=part_recv_sem.at[step],
            device_id={"cell": lax.rem(me + step, n)},
            device_id_type=MESH,
        )

    part[...] = jnp.sum(squares[...].reshape(*part.shape, LANES), axis=-1)

    @pl.loop(1, n)
    def _(step):
        copy_part(step).start()

    slots[0] = part[...]

    @pl.loop(0, chunks)
    def _(chunk):
        out(chunk).wait()

    @pl.loop(1, n)
    def _(step):
        copy_part(step).wait()

    total[...] = jnp.sum(slots[...], axis=0)


def sensitivities(fields, quads, cell_values, n):
    comps, rows, _ = fields.shape
    chunks = cell_values[0].shape[0]
    electrodes, readings, cells = rows * n, quads.shape[1], chunks * LANES
    sums = (readings // LANES, LANES)
    in_vmem = pl.BlockSpec(memory_space=pltpu.VMEM)
    anywhere = pl.BlockSpec(memory_space=pl.ANY)
    return pl.pallas_call(
        functools.partial(exchange_kernel, n),
        out_shape=[
            jax.ShapeDtypeStruct((readings * 4, cells), jnp.float32),
            jax.ShapeDtypeStruct(sums, jnp.float32),
        ],
        in_specs=[pl.BlockSpec(memory_space=pltpu.SMEM), anywhere] + [in_vmem] * len(cell_values),
        out_specs=[anywhere, in_vmem],
        scratch_shapes=[
            pltpu.VMEM((chunks, comps, electrodes, LANES), fields.dtype),
            pltpu.VMEM((chunks, readings * 4, LANES), jnp.float32),
            pltpu.VMEM((comps, electrodes, LANES), jnp.float32),
            pltpu.VMEM((2 * comps, readings, LANES), jnp.float32),
            pltpu.VMEM((readings, LANES), jnp.float32),
            pltpu.VMEM((24, chunks, LANES), jnp.float32),
            pltpu.VMEM(sums, jnp.float32),
            pltpu.VMEM((n, *sums), jnp.float32),
            pltpu.SemaphoreType.DMA((chunks, n)),
            pltpu.SemaphoreType.DMA((chunks, n)),
            pltpu.SemaphoreType.DMA((chunks,)),
            pltpu.SemaphoreType.DMA((chunks,)),
            pltpu.SemaphoreType.DMA((n,)),
            pltpu.SemaphoreType.DMA((n,)),
        ],
        compiler_params=pltpu.CompilerParams(
            collective_id=0, has_side_effects=True, vmem_limit_bytes=56 * 2**20
        ),
        name="exchange",
    )(quads, fields, *cell_values)


def norm_kernel(sens, scale, jacobian, coverage):
    count = sens.shape[0]

    @pl.when(pl.program_id(0) == 0)
    def _():
        coverage[...] = jnp.zeros_like(coverage)

    for lane in range(sens.shape[1] // LANES):
        at = pl.ds(lane * LANES, LANES)
        normed = sens[:, at] * scale[...]
        jacobian[:, :, at] = normed.reshape(count // 4, 4, LANES).astype(jnp.bfloat16)
        coverage[:, at] += jnp.sum((normed * normed).reshape(count // 8, 8, LANES), axis=0)


def normalise(sens, scale):
    rows, cells = sens.shape
    block = 1024
    return pl.pallas_call(
        norm_kernel,
        grid=(rows // block,),
        in_specs=[
            pl.BlockSpec((block, cells), lambda i: (i, 0)),
            pl.BlockSpec((block, LANES), lambda i: (i, 0)),
        ],
        out_specs=[
            pl.BlockSpec((block // 4, 4, cells), lambda i: (i, 0, 0)),
            pl.BlockSpec((8, cells), lambda i: (0, 0)),
        ],
        out_shape=[
            jax.ShapeDtypeStruct((rows // 4, 4, cells), jnp.bfloat16),
            jax.ShapeDtypeStruct((8, cells), jnp.float32),
        ],
        compiler_params=pltpu.CompilerParams(vmem_limit_bytes=48 * 2**20),
        name="norm",
    )(sens, scale)


def local(fields, horiz, vertical, tilt_angle, azimuth, electrode_quads):
    shards = lax.axis_size("cell")
    cells = horiz.shape[0]
    readings = electrode_quads.shape[0]
    values = (
        horiz, vertical, jnp.sin(tilt_angle), jnp.cos(tilt_angle), jnp.sin(azimuth), jnp.cos(azimuth)
    )
    sens, total = sensitivities(
        fields.transpose(1, 0, 2),
        electrode_quads.T,
        [x.reshape(cells // LANES, LANES) for x in values],
        shards,
    )
    meansq = total.reshape(-1) / (4.0 * cells * shards)
    scale = jnp.broadcast_to(lax.rsqrt(meansq + 1e-06)[:, None, None], (readings, 4, LANES))
    jacobian, coverage = normalise(sens, scale.reshape(readings * 4, LANES))
    return jacobian, jnp.sum(coverage, axis=0)


def solution(mesh):
    placed = (
        P(("grp", "cell"), None, None),
        P(("grp", "cell")),
        P(("grp", "cell")),
        P(("grp", "cell")),
        P(("grp", "cell")),
        P("grp", None),
    )
    return jax.shard_map(
        local,
        mesh=mesh,
        in_specs=placed,
        out_specs=(P("grp", None, "cell"), P(("grp", "cell"))),
        check_vma=False,
    )
```

profile of v0, /device:TPU:0, one launch (start us, length us, event | category | flops | bytes accessed | tf_op | source)
XLA Modules:
  0.0 323.3 jit_solution(2146307126289838958)
XLA Ops:
  0.6 1.3 cosine_bitcast_fusion
  2.0 305.8 %exchange.1 = (f32[8192,512]{1,0:T(8,128)}, f32[16,128]{1,0:T(8,128)}) custom-call(s32[4,2048]{1,0:T(4,128)} %bitcast.15, bf16[3,256,8192]{2,1,0:T(8,128)(2,1)} %bitcast.14, f32[4,128]{1,0:T(4,128)} %bitcast.16, f32[4,128]{1,0:T(4,128)} %bitcast.17, f32[4,128]{1,0:T(4,128)} %get-tuple-element.14.sin_t, f32[4,128]{1,0:T(4,128)} %get-tuple-element.15.cos_t, ...), custom_call_target="tpu_custom_call" | custom-call | tf_op jit(solution)/shard_map/exchange/pallas_call | solution.py:175
  307.8 0.7 rsqrt_bitcast_fusion
  308.5 0.3 broadcast_in_dim.10
  308.8 0.6 broadcast_in_dim.11
  309.4 1.1 broadcast_in_dim.12.scale
  310.6 12.2 %norm.1 = (bf16[2048,4,512]{2,1,0:T(4,128)(2,1)}, f32[8,512]{1,0:T(8,128)S(1)}) custom-call(f32[8192,512]{1,0:T(8,128)} %get-tuple-element.6.sens, f32[8192,128]{1,0:T(8,128)S(1)} %broadcast_in_dim.12.scale), custom_call_target="tpu_custom_call" | custom-call | tf_op jit(solution)/shard_map/norm/pallas_call | solution.py:223
  322.8 0.6 reduce_sum.9
where the time goes:
time: 324 us; the launch traced here: 323 us
  Pallas kernels  318 us (98%)
  local copies, waits for them, and re-layouts  3.45 us (1%)
    pallas_call x1, Pallas kernels, sensitivities(): pl.pallas_call(functools.partial(exchange_kernel, n), out_shape=[jax.Shap...  306 us
    pallas_call x1, Pallas kernels, normalise(): pl.pallas_call(norm_kernel, grid=(rows // block,), in_specs=[pl.BlockSpec...  12.2 us

commit v1 on v0

v1 whole, which is shorter than its diff:
```python
import functools

import jax
import jax.numpy as jnp
from jax import lax
from jax.experimental import pallas as pl
from jax.experimental.pallas import tpu as pltpu
from jax.sharding import PartitionSpec as P

MESH = pl.DeviceIdType.MESH
LANES = 128
DEPTH = 256
UNROLL = 16
TILE = 1024


def greet(n, me):
    barrier = pltpu.get_barrier_semaphore()

    @pl.loop(1, n)
    def _(step):
        pl.semaphore_signal(barrier, inc=1, device_id={"cell": lax.rem(me + step, n)}, device_id_type=MESH)

    pl.semaphore_wait(barrier, n - 1)


def fill_coefficients(coef, horiz, vertical, tilt_angle, azimuth):
    sin_t, cos_t = jnp.sin(tilt_angle), jnp.cos(tilt_angle)
    sin_p, cos_p = jnp.sin(azimuth), jnp.cos(azimuth)
    rows = (
        sin_t * cos_p, sin_t * sin_p, cos_t,
        cos_t * cos_p, cos_t * sin_p, -sin_t,
        -sin_t * sin_p, sin_t * cos_p,
        -horiz, -vertical, horiz - vertical,
    )
    for k, row in enumerate(rows):
        coef[k] = row


def spread_quads(quads, block_of, place_of):
    for k in range(4):
        @pl.loop(0, quads.shape[1] // LANES)
        def _(i):
            at = pl.multiple_of(i * LANES, LANES)
            row = quads[pl.ds(k, 1), pl.ds(at, LANES)]
            block = row // DEPTH
            for target, value in ((block_of, block), (place_of, row - block * DEPTH)):
                wide = jnp.broadcast_to(value.astype(jnp.float32), (LANES, LANES))
                target[k, pl.ds(at, LANES), :] = wide.T.astype(jnp.bfloat16)


def add_group(chunk, group, landed, block_of, place_of, diffs):
    readings = diffs.shape[1]
    lane = lax.broadcasted_iota(jnp.int32, (TILE, LANES), 1).astype(jnp.float32)
    lanes = [(lane + LANES * h).astype(jnp.bfloat16) for h in range(DEPTH // LANES)]
    here = jnp.full((TILE, LANES), group, jnp.int32).astype(jnp.float32).astype(jnp.bfloat16)
    one, none = jnp.bfloat16(1), jnp.bfloat16(0)
    away = jnp.bfloat16(-1)

    @pl.loop(0, readings // TILE)
    def _(t):
        at = pl.multiple_of(t * TILE, TILE)
        rows = pl.ds(pl.multiple_of(group * DEPTH, DEPTH), DEPTH)
        grads = jnp.concatenate([landed[chunk, c, rows, :] for c in range(3)], axis=-1)
        for pair in range(2):
            plus, minus = (
                jnp.where(block_of[k, pl.ds(at, TILE), :] == here, place_of[k, pl.ds(at, TILE), :], away)
                for k in (2 * pair, 2 * pair + 1)
            )
            select = jnp.concatenate(
                [jnp.where(plus == x, one, jnp.where(minus == x, -one, none)) for x in lanes], axis=-1
            )
            out = jnp.dot(select, grads, preferred_element_type=jnp.float32)
            for c in range(3):
                diffs[3 * pair + c, pl.ds(at, TILE), :] += out[:, c * LANES:(c + 1) * LANES]


def chunk_sensitivities(chunk, coef, diffs, sens, squares):
    readings = squares.shape[0]
    tile = 32

    @pl.loop(0, readings // tile)
    def _(i):
        at = pl.multiple_of(i * tile, tile)
        s = [diffs[c, pl.ds(at, tile), :] for c in range(3)]
        r = [diffs[3 + c, pl.ds(at, tile), :] for c in range(3)]
        k = [coef[j, pl.ds(chunk, 1), :] for j in range(11)]
        sn, rn = (f[0] * k[0] + f[1] * k[1] + f[2] * k[2] for f in (s, r))
        st, rt = (f[0] * k[3] + f[1] * k[4] + f[2] * k[5] for f in (s, r))
        sp, rp = (f[0] * k[6] + f[1] * k[7] for f in (s, r))
        dot = s[0] * r[0] + s[1] * r[1] + s[2] * r[2]
        both = sn * rn
        values = (
            k[8] * (dot - both), k[9] * both, k[10] * (st * rn + sn * rt), k[10] * (sp * rn + sn * rp)
        )
        square = squares[pl.ds(at, tile), :]
        for p, value in enumerate(values):
            sens[chunk, pl.ds(4 * at + p, tile, stride=4), :] = value
            square = square + value * value
        squares[pl.ds(at, tile), :] = square


def flip(a, b, n):
    out, weight = 0, 1
    while weight < n:
        out = out + (a // weight + b // weight) % 2 * weight
        weight *= 2
    return out


def exchange_kernel(
    n, quads_hbm, fields, horiz, vertical, tilt_angle, azimuth, sens, total,
    landed, diffs, squares, coef, cells_of, quads, block_of, place_of, part, slots,
    send_sem, recv_sem, own_sem, small_sem, part_send_sem, part_recv_sem,
):
    me = lax.axis_index("cell")
    rows = fields.shape[1]
    chunks = landed.shape[0]
    readings = squares.shape[0]
    cells = chunks * LANES
    groups = rows * n // DEPTH
    members = DEPTH // rows
    my_group = me // members
    paired = n & (n - 1) == 0
    greet(n, me)

    def landing(chunk):
        return landed.at[chunk, :, pl.ds(pl.multiple_of(me * rows, rows), rows), :]

    def leaving(device, chunk):
        return fields.at[:, :, pl.ds(pl.multiple_of(device * cells + chunk * LANES, LANES), LANES)]

    def copy(chunk, peer, source):
        return pltpu.make_async_remote_copy(
            src_ref=leaving(peer, chunk),
            dst_ref=landing(chunk),
            send_sem=send_sem.at[chunk, peer],
            recv_sem=recv_sem.at[chunk, source],
            device_id={"cell": peer},
            device_id_type=MESH,
        )

    def own(chunk):
        return pltpu.make_async_copy(leaving(me, chunk), landing(chunk), own_sem.at[chunk])

    def partner(chunk, step):
        around = lax.rem(me + step, n)
        if not paired:
            return around
        last = (chunk + 1) // chunks
        across = flip(me, step % 2 * (n // 2) + step // 2, n)
        return last * across + (1 - last) * around

    def turn_group(chunk, turn):
        around = lax.rem(my_group - turn + groups, groups)
        if not paired:
            return around
        last = (chunk + 1) // chunks
        return last * flip(my_group, turn, groups) + (1 - last) * around

    @pl.loop(0, chunks)
    def _(chunk):
        @pl.loop(1, n)
        def _(step):
            copy(chunk, partner(chunk, step), me).start()

        own(chunk).start()

    smalls = [pltpu.make_async_copy(quads_hbm, quads, small_sem.at[4])] + [
        pltpu.make_async_copy(x, cells_of.at[k], small_sem.at[k])
        for k, x in enumerate((horiz, vertical, tilt_angle, azimuth))
    ]
    for small in smalls:
        small.start()
    squares[...] = jnp.zeros_like(squares)
    for small in smalls:
        small.wait()
    fill_coefficients(coef, *(cells_of[k] for k in range(4)))
    spread_quads(quads, block_of, place_of)

    @pl.loop(0, chunks)
    def _(chunk):
        @pl.loop(0, readings // LANES)
        def _(i):
            at = pl.multiple_of(i * LANES, LANES)
            for c in range(6):
                diffs[c, pl.ds(at, LANES), :] = jnp.zeros((LANES, LANES), jnp.float32)

        @pl.loop(0, groups)
        def _(turn):
            group = turn_group(chunk, turn)

            @pl.loop(0, members)
            def _(k):
                source = group * members + k

                @pl.when(source == me)
                def _():
                    own(chunk).wait()

                @pl.when(source != me)
                def _():
                    copy(chunk, source, source).wait_recv()

            add_group(chunk, group, landed, block_of, place_of, diffs)

        chunk_sensitivities(chunk, coef, diffs, sens, squares)

    def copy_part(step):
        return pltpu.make_async_remote_copy(
            src_ref=part,
            dst_ref=slots.at[step],
            send_sem=part_send_sem.at[step],
            recv_sem=part_recv_sem.at[step],
            device_id={"cell": lax.rem(me + step, n)},
            device_id_type=MESH,
        )

    depth = readings // LANES
    lane = lax.broadcasted_iota(jnp.int32, (depth, LANES), 1)

    def gather_sum(j, packed):
        at = pl.multiple_of(j * depth, depth)
        return jnp.where(lane == j, jnp.sum(squares[pl.ds(at, depth), :], axis=-1, keepdims=True), packed)

    part[...] = lax.fori_loop(0, LANES, gather_sum, jnp.zeros((depth, LANES), jnp.float32), unroll=8)

    @pl.loop(1, n)
    def _(step):
        copy_part(step).start()

    slots[0] = part[...]

    @pl.loop(0, chunks)
    def _(chunk):
        @pl.loop(1, n)
        def _(step):
            copy(chunk, lax.rem(me + step, n), me).wait_send()

    @pl.loop(1, n)
    def _(step):
        copy_part(step).wait()

    total[...] = jnp.sum(slots[...], axis=0)


def sensitivities(fields, quads, cell_values, n):
    comps, rows, _ = fields.shape
    chunks = cell_values[0].shape[0]
    electrodes, readings = rows * n, quads.shape[1]
    sums = (readings // LANES, LANES)
    in_vmem = pl.BlockSpec(memory_space=pltpu.VMEM)
    anywhere = pl.BlockSpec(memory_space=pl.ANY)
    return pl.pallas_call(
        functools.partial(exchange_kernel, n),
        out_shape=[
            pltpu.VMEM((chunks, readings * 4, LANES), jnp.float32),
            jax.ShapeDtypeStruct(sums, jnp.float32),
        ],
        in_specs=[anywhere] * (2 + len(cell_values)),
        out_specs=[in_vmem, in_vmem],
        scratch_shapes=[
            pltpu.VMEM((chunks, comps, electrodes, LANES), fields.dtype),
            pltpu.VMEM((2 * comps, readings, LANES), jnp.float32),
            pltpu.VMEM((readings, LANES), jnp.float32),
            pltpu.VMEM((11, chunks, LANES), jnp.float32),
            pltpu.VMEM((4, chunks, LANES), jnp.float32),
            pltpu.VMEM(quads.shape, quads.dtype),
            pltpu.VMEM((4, readings, LANES), jnp.bfloat16),
            pltpu.VMEM((4, readings, LANES), jnp.bfloat16),
            pltpu.VMEM(sums, jnp.float32),
            pltpu.VMEM((n, *sums), jnp.float32),
            pltpu.SemaphoreType.DMA((chunks, n)),
            pltpu.SemaphoreType.DMA((chunks, n)),
            pltpu.SemaphoreType.DMA((chunks,)),
            pltpu.SemaphoreType.DMA((5,)),
            pltpu.SemaphoreType.DMA((n,)),
            pltpu.SemaphoreType.DMA((n,)),
        ],
        compiler_params=pltpu.CompilerParams(
            collective_id=0, has_side_effects=True, vmem_limit_bytes=40 * 2**20
        ),
        name="exchange",
    )(quads, fields, *cell_values)


def norm_kernel(count, sens, total, jacobian, coverage, scale):
    depth = total.shape[0]
    readings, _, cells = jacobian.shape
    step = pl.program_id(0)

    @pl.when(step == 0)
    def _():
        coverage[...] = jnp.zeros_like(coverage)
        value = lax.rsqrt(total[...] / count + 1e-06)
        for p in range(4):
            scale[pl.ds(p, depth, stride=4), :] = value

    wide = 4 * depth
    lane = lax.broadcasted_iota(jnp.int32, (wide, LANES), 1)

    first = step * (readings // depth)

    def some(g, sums):
        columns = [
            jnp.sum(jnp.where(lane == first + UNROLL * g + u, scale[...], 0.0), axis=-1, keepdims=True)
            for u in range(UNROLL)
        ]
        for u in range(UNROLL):
            i = UNROLL * g + u
            rows = pl.ds(pl.multiple_of((first + i) * wide, wide), wide)
            put = pl.ds(pl.multiple_of(i * depth, depth), depth)
            for c in range(cells // LANES):
                normed = sens[c, rows, :] * columns[u]
                jacobian[put, :, pl.ds(c * LANES, LANES)] = normed.reshape(depth, 4, LANES).astype(jnp.bfloat16)
                square = jnp.sum((normed * normed).reshape(wide // 8, 8, LANES), axis=0)
                sums = sums[:c] + (sums[c] + square,) + sums[c + 1:]
        return sums

    sums = lax.fori_loop(
        0, readings // depth // UNROLL, some,
        tuple(coverage[:, pl.ds(c * LANES, LANES)] for c in range(cells // LANES)),
    )
    for c, total_of in enumerate(sums):
        coverage[:, pl.ds(c * LANES, LANES)] = total_of


def normalise(sens, total, count):
    chunks, rows, _ = sens.shape
    readings, cells = rows // 4, chunks * LANES
    block = 512
    return pl.pallas_call(
        functools.partial(norm_kernel, count),
        grid=(readings // block,),
        in_specs=[
            pl.BlockSpec(memory_space=pltpu.VMEM),
            pl.BlockSpec(memory_space=pltpu.VMEM),
        ],
        out_specs=[
            pl.BlockSpec((block, 4, cells), lambda i: (i, 0, 0)),
            pl.BlockSpec((8, cells), lambda i: (0, 0)),
        ],
        out_shape=[
            jax.ShapeDtypeStruct((readings, 4, cells), jnp.bfloat16),
            jax.ShapeDtypeStruct((8, cells), jnp.float32),
        ],
        scratch_shapes=[pltpu.VMEM((4 * total.shape[0], LANES), jnp.float32)],
        compiler_params=pltpu.CompilerParams(vmem_limit_bytes=8 * 2**20),
        name="norm",
    )(pltpu.with_memory_space_constraint(sens, pltpu.VMEM), total)


def local(fields, horiz, vertical, tilt_angle, azimuth, electrode_quads):
    shards = lax.axis_size("cell")
    cells = horiz.shape[0]
    sens, total = sensitivities(
        fields.transpose(1, 0, 2),
        electrode_quads.T,
        [x.reshape(cells // LANES, LANES) for x in (horiz, vertical, tilt_angle, azimuth)],
        shards,
    )
    jacobian, coverage = normalise(sens, total, 4.0 * cells * shards)
    return jacobian, jnp.sum(coverage, axis=0)


def solution(mesh):
    placed = (
        P(("grp", "cell"), None, None),
        P(("grp", "cell")),
        P(("grp", "cell")),
        P(("grp", "cell")),
        P(("grp", "cell")),
        P("grp", None),
    )
    return jax.shard_map(
        local,
        mesh=mesh,
        in_specs=placed,
        out_specs=(P("grp", None, "cell"), P(("grp", "cell"))),
        check_vma=False,
    )
```

time: 324 us -> 302 us (0.932)
  Pallas kernels: 318 us -> 300 us
    pallas_call x2, Pallas kernels: 318 us -> 300 us  [the longest x1 294 us: sensitivities(): pl.pallas_call(functools.partial(exchange_kernel, n), out_shape=[pltpu.VM...]
where the time goes in v1:
time: 302 us
  Pallas kernels  300 us (99%)
    pallas_call x1, Pallas kernels, sensitivities(): pl.pallas_call(functools.partial(exchange_kernel, n), out_shape=[pltpu.VM...  294 us

profile of v1, /device:TPU:0, one launch (start us, length us, event | category | flops | bytes accessed | tf_op | source)
XLA Modules:
  0.0 302.1 jit_solution(5523113363130895270)
XLA Ops:
  0.6 294.4 %exchange.1 = (f32[4,8192,128]{2,1,0:T(8,128)S(1)}, f32[16,128]{1,0:T(8,128)}) custom-call(s32[4,2048]{1,0:T(4,128)} %bitcast.7, bf16[3,256,8192]{2,1,0:T(8,128)(2,1)} %bitcast.6, f32[4,128]{1,0:T(4,128)} %bitcast.8, f32[4,128]{1,0:T(4,128)} %bitcast.9, f32[4,128]{1,0:T(4,128)} %bitcast.10, f32[4,128]{1,0:T(4,128)} %bitcast.11), custom_call_target="tpu_custom_call" | custom-call | tf_op jit(solution)/shard_map/exchange/pallas_call | solution.py:254
  295.0 0.0 copy-start
  295.0 0.7 copy-done
  295.7 5.8 %norm.1 = (bf16[2048,4,512]{2,1,0:T(4,128)(2,1)}, f32[8,512]{1,0:T(8,128)S(1)}) custom-call(f32[4,8192,128]{2,1,0:T(8,128)S(1)} %get-tuple-element.6.sens, f32[16,128]{1,0:T(8,128)S(1)} %copy-done), custom_call_target="tpu_custom_call" | custom-call | tf_op jit(solution)/shard_map/norm/pallas_call | solution.py:332
  301.5 0.6 reduce_sum.9
Async XLA Ops:
  295.0 0.7 copy-start

commit v2 on v1

--- a/solution.py
+++ b/solution.py
@@ -50,7 +50,7 @@
 
 
 def add_group(chunk, group, landed, block_of, place_of, diffs):
-    readings = diffs.shape[1]
+    readings = diffs.shape[2]
     lane = lax.broadcasted_iota(jnp.int32, (TILE, LANES), 1).astype(jnp.float32)
     lanes = [(lane + LANES * h).astype(jnp.bfloat16) for h in range(DEPTH // LANES)]
     here = jnp.full((TILE, LANES), group, jnp.int32).astype(jnp.float32).astype(jnp.bfloat16)
@@ -72,7 +72,7 @@
             )
             out = jnp.dot(select, grads, preferred_element_type=jnp.float32)
             for c in range(3):
-                diffs[3 * pair + c, pl.ds(at, TILE), :] += out[:, c * LANES:(c + 1) * LANES]
+                diffs[chunk % 2, 3 * pair + c, pl.ds(at, TILE), :] += out[:, c * LANES:(c + 1) * LANES]
 
 
 def chunk_sensitivities(chunk, coef, diffs, sens, squares):
@@ -82,8 +82,8 @@
     @pl.loop(0, readings // tile)
     def _(i):
         at = pl.multiple_of(i * tile, tile)
-        s = [diffs[c, pl.ds(at, tile), :] for c in range(3)]
-        r = [diffs[3 + c, pl.ds(at, tile), :] for c in range(3)]
+        s = [diffs[chunk % 2, c, pl.ds(at, tile), :] for c in range(3)]
+        r = [diffs[chunk % 2, 3 + c, pl.ds(at, tile), :] for c in range(3)]
         k = [coef[j, pl.ds(chunk, 1), :] for j in range(11)]
         sn, rn = (f[0] * k[0] + f[1] * k[1] + f[2] * k[2] for f in (s, r))
         st, rt = (f[0] * k[3] + f[1] * k[4] + f[2] * k[5] for f in (s, r))
@@ -151,12 +151,18 @@
         across = flip(me, step % 2 * (n // 2) + step // 2, n)
         return last * across + (1 - last) * around
 
+    half = groups // 2
+    upper = my_group // max(half, 1)
+
     def turn_group(chunk, turn):
-        around = lax.rem(my_group - turn + groups, groups)
         if not paired:
-            return around
+            return lax.rem(my_group - turn + groups, groups)
+        across = flip(my_group, turn, groups)
+        far = turn // half
         last = (chunk + 1) // chunks
-        return last * flip(my_group, turn, groups) + (1 - last) * around
+        inward = upper * (turn - half) + (1 - upper) * (groups - 1 - (turn - half))
+        direct = far * (1 - last)
+        return direct * inward + (1 - direct) * across
 
     @pl.loop(0, chunks)
     def _(chunk):
@@ -178,41 +184,53 @@
     fill_coefficients(coef, *(cells_of[k] for k in range(4)))
     spread_quads(quads, block_of, place_of)
 
-    @pl.loop(0, chunks)
-    def _(chunk):
+    def take(chunk, first, count):
+        @pl.loop(0, count)
+        def _(turn):
+            group = turn_group(chunk, first + turn)
+
+            @pl.loop(0, members)
+            def _(k):
+                source = group * members + k
+
+                @pl.when(source == me)
+                def _():
+                    own(chunk).wait()
+
+                @pl.when(source != me)
+                def _():
+                    copy(chunk, source, source).wait_recv()
+
+            add_group(chunk, group, landed, block_of, place_of, diffs)
+
+    def take_near(chunk):
         @pl.loop(0, readings // LANES)
         def _(i):
             at = pl.multiple_of(i * LANES, LANES)
             for c in range(6):
-                diffs[c, pl.ds(at, LANES), :] = jnp.zeros((LANES, LANES), jnp.float32)
-
-        @pl.loop(0, groups)
-        def _(turn):
-            group = turn_group(chunk, turn)
-
-            @pl.loop(0, members)
-            def _(k):
-                source = group * members + k
-
-                @pl.when(source == me)
-                def _():
-                    own(chunk).wait()
-
-                @pl.when(source != me)
-                def _():
-                    copy(chunk, source, source).wait_recv()
-
-            add_group(chunk, group, landed, block_of, place_of, diffs)
-
+                diffs[chunk % 2, c, pl.ds(at, LANES), :] = jnp.zeros((LANES, LANES), jnp.float32)
+
+        take(chunk, 0, half)
+
+    take_near(0)
+
+    @pl.loop(0, chunks)
+    def _(chunk):
+        @pl.when(chunk + 1 < chunks)
+        def _():
+            take_near(chunk + 1)
+
+        take(chunk, half, groups - half)
         chunk_sensitivities(chunk, coef, diffs, sens, squares)
 
     def copy_part(step):
+        peer = flip(me, n - step, n) if paired else lax.rem(me + n - step, n)
         return pltpu.make_async_remote_copy(
             src_ref=part,
             dst_ref=slots.at[step],
             send_sem=part_send_sem.at[step],
             recv_sem=part_recv_sem.at[step],
-            device_id={"cell": lax.rem(me + step, n)},
+            device_id={"cell": peer},
             device_id_type=MESH,
         )
 
@@ -223,7 +241,7 @@
         at = pl.multiple_of(j * depth, depth)
         return jnp.where(lane == j, jnp.sum(squares[pl.ds(at, depth), :], axis=-1, keepdims=True), packed)
 
-    part[...] = lax.fori_loop(0, LANES, gather_sum, jnp.zeros((depth, LANES), jnp.float32), unroll=8)
+    part[...] = lax.fori_loop(0, LANES, gather_sum, jnp.zeros((depth, LANES), jnp.float32), unroll=32)
 
     @pl.loop(1, n)
     def _(step):
@@ -255,13 +273,13 @@
         functools.partial(exchange_kernel, n),
         out_shape=[
             pltpu.VMEM((chunks, readings * 4, LANES), jnp.float32),
-            jax.ShapeDtypeStruct(sums, jnp.float32),
+            pltpu.VMEM(sums, jnp.float32),
         ],
         in_specs=[anywhere] * (2 + len(cell_values)),
         out_specs=[in_vmem, in_vmem],
         scratch_shapes=[
             pltpu.VMEM((chunks, comps, electrodes, LANES), fields.dtype),
-            pltpu.VMEM((2 * comps, readings, LANES), jnp.float32),
+            pltpu.VMEM((2, 2 * comps, readings, LANES), jnp.float32),
             pltpu.VMEM((readings, LANES), jnp.float32),
             pltpu.VMEM((11, chunks, LANES), jnp.float32),
             pltpu.VMEM((4, chunks, LANES), jnp.float32),
@@ -284,14 +302,14 @@
     )(quads, fields, *cell_values)
 
 
-def norm_kernel(count, sens, total, jacobian, coverage, scale):
+def norm_kernel(count, sens, total, jacobian, coverage, scale, sums_of):
     depth = total.shape[0]
     readings, _, cells = jacobian.shape
     step = pl.program_id(0)
 
     @pl.when(step == 0)
     def _():
-        coverage[...] = jnp.zeros_like(coverage)
+        sums_of[...] = jnp.zeros_like(sums_of)
         value = lax.rsqrt(total[...] / count + 1e-06)
         for p in range(4):
             scale[pl.ds(p, depth, stride=4), :] = value
@@ -319,10 +337,15 @@
 
     sums = lax.fori_loop(
         0, readings // depth // UNROLL, some,
-        tuple(coverage[:, pl.ds(c * LANES, LANES)] for c in range(cells // LANES)),
+        tuple(sums_of[c] for c in range(cells // LANES)),
     )
     for c, total_of in enumerate(sums):
-        coverage[:, pl.ds(c * LANES, LANES)] = total_of
+        sums_of[c] = total_of
+
+    @pl.when(step == pl.num_programs(0) - 1)
+    def _():
+        for c in range(cells // LANES):
+            coverage[pl.ds(c, 1), :] = jnp.sum(sums_of[c], axis=0, keepdims=True)
 
 
 def normalise(sens, total, count):
@@ -338,16 +361,19 @@
         ],
         out_specs=[
             pl.BlockSpec((block, 4, cells), lambda i: (i, 0, 0)),
-            pl.BlockSpec((8, cells), lambda i: (0, 0)),
+            pl.BlockSpec((chunks, LANES), lambda i: (0, 0)),
         ],
         out_shape=[
             jax.ShapeDtypeStruct((readings, 4, cells), jnp.bfloat16),
-            jax.ShapeDtypeStruct((8, cells), jnp.float32),
-        ],
-        scratch_shapes=[pltpu.VMEM((4 * total.shape[0], LANES), jnp.float32)],
+            jax.ShapeDtypeStruct((chunks, LANES), jnp.float32),
+        ],
+        scratch_shapes=[
+            pltpu.VMEM((4 * total.shape[0], LANES), jnp.float32),
+            pltpu.VMEM((chunks, 8, LANES), jnp.float32),
+        ],
         compiler_params=pltpu.CompilerParams(vmem_limit_bytes=8 * 2**20),
         name="norm",
-    )(pltpu.with_memory_space_constraint(sens, pltpu.VMEM), total)
+    )(*(pltpu.with_memory_space_constraint(x, pltpu.VMEM) for x in (sens, total)))
 
 
 def local(fields, horiz, vertical, tilt_angle, azimuth, electrode_quads):
@@ -360,7 +386,7 @@
         shards,
     )
     jacobian, coverage = normalise(sens, total, 4.0 * cells * shards)
-    return jacobian, jnp.sum(coverage, axis=0)
+    return jacobian, coverage.reshape(-1)
 
 
 def solution(mesh):

time: 302 us -> 297 us (0.983)
  Pallas kernels: 300 us -> 296 us
    pallas_call x1, Pallas kernels: 294 us -> 290 us  [sensitivities(): pl.pallas_call(functools.partial(exchange_kernel, n), out_shape=[pltpu.VM...]
where the time goes in v2:
time: 297 us; the launch traced here: 296 us
  Pallas kernels  296 us (100%)
    pallas_call x1, Pallas kernels, sensitivities(): pl.pallas_call(functools.partial(exchange_kernel, n), out_shape=[pltpu.VM...  290 us

profile of v2, /device:TPU:0, one launch (start us, length us, event | category | flops | bytes accessed | tf_op | source)
XLA Modules:
  0.0 296.4 jit_solution(17554137913907767076)
XLA Ops:
  0.6 289.9 %exchange.1 = (f32[4,8192,128]{2,1,0:T(8,128)S(1)}, f32[16,128]{1,0:T(8,128)S(1)}) custom-call(s32[4,2048]{1,0:T(4,128)} %bitcast.8, bf16[3,256,8192]{2,1,0:T(8,128)(2,1)} %bitcast.7, f32[4,128]{1,0:T(4,128)} %bitcast.9, f32[4,128]{1,0:T(4,128)} %bitcast.10, f32[4,128]{1,0:T(4,128)} %bitcast.11, f32[4,128]{1,0:T(4,128)} %bitcast.12), custom_call_target="tpu_custom_call" | custom-call | tf_op jit(solution)/shard_map/exchange/pallas_call | solution.py:272
  290.5 5.9 %norm.1 = (bf16[2048,4,512]{2,1,0:T(4,128)(2,1)}, f32[4,128]{1,0:T(4,128)}) custom-call(f32[4,8192,128]{2,1,0:T(8,128)S(1)} %get-tuple-element.6.sens, f32[16,128]{1,0:T(8,128)S(1)} %get-tuple-element.7.total), custom_call_target="tpu_custom_call" | custom-call | tf_op jit(solution)/shard_map/norm/pallas_call | solution.py:355

commit v3 on v2

--- a/solution.py
+++ b/solution.py
@@ -10,6 +10,8 @@
 MESH = pl.DeviceIdType.MESH
 LANES = 128
 DEPTH = 256
+PARTS = 8
+SLOTS = 4
 UNROLL = 16
 TILE = 1024
 
@@ -111,7 +113,7 @@
 def exchange_kernel(
     n, quads_hbm, fields, horiz, vertical, tilt_angle, azimuth, sens, total,
     landed, diffs, squares, coef, cells_of, quads, block_of, place_of, part, slots,
-    send_sem, recv_sem, own_sem, small_sem, part_send_sem, part_recv_sem,
+    send_sem, recv_sem, own_sem, small_sem, part_sem,
 ):
     me = lax.axis_index("cell")
     rows = fields.shape[1]
@@ -134,7 +136,7 @@
         return pltpu.make_async_remote_copy(
             src_ref=leaving(peer, chunk),
             dst_ref=landing(chunk),
-            send_sem=send_sem.at[chunk, peer],
+            send_sem=send_sem.at[chunk],
             recv_sem=recv_sem.at[chunk, source],
             device_id={"cell": peer},
             device_id_type=MESH,
@@ -228,8 +230,8 @@
         return pltpu.make_async_remote_copy(
             src_ref=part,
             dst_ref=slots.at[step],
-            send_sem=part_send_sem.at[step],
-            recv_sem=part_recv_sem.at[step],
+            send_sem=part_sem.at[0],
+            recv_sem=part_sem.at[1],
             device_id={"cell": peer},
             device_id_type=MESH,
         )
@@ -249,15 +251,15 @@
 
     slots[0] = part[...]
 
+    def wait_bytes(ref, sem):
+        pltpu.make_async_copy(ref, ref, sem).wait()
+
     @pl.loop(0, chunks)
     def _(chunk):
-        @pl.loop(1, n)
-        def _(step):
-            copy(chunk, lax.rem(me + step, n), me).wait_send()
-
-    @pl.loop(1, n)
-    def _(step):
-        copy_part(step).wait()
+        wait_bytes(landed.at[chunk, :, pl.ds(0, rows * (n - 1)), :], send_sem.at[chunk])
+
+    for k in range(2):
+        wait_bytes(slots.at[pl.ds(1, n - 1)], part_sem.at[k])
 
     total[...] = jnp.sum(slots[...], axis=0)
 
@@ -288,12 +290,11 @@
             pltpu.VMEM((4, readings, LANES), jnp.bfloat16),
             pltpu.VMEM(sums, jnp.float32),
             pltpu.VMEM((n, *sums), jnp.float32),
-            pltpu.SemaphoreType.DMA((chunks, n)),
+            pltpu.SemaphoreType.DMA((chunks,)),
             pltpu.SemaphoreType.DMA((chunks, n)),
             pltpu.SemaphoreType.DMA((chunks,)),
             pltpu.SemaphoreType.DMA((5,)),
-            pltpu.SemaphoreType.DMA((n,)),
-            pltpu.SemaphoreType.DMA((n,)),
+            pltpu.SemaphoreType.DMA((2,)),
         ],
         compiler_params=pltpu.CompilerParams(
             collective_id=0, has_side_effects=True, vmem_limit_bytes=40 * 2**20
@@ -302,74 +303,76 @@
     )(quads, fields, *cell_values)
 
 
-def norm_kernel(count, sens, total, jacobian, coverage, scale, sums_of):
+def norm_kernel(count, sens, total, jacobian, coverage, scale, staged, out_sem):
     depth = total.shape[0]
     readings, _, cells = jacobian.shape
-    step = pl.program_id(0)
-
-    @pl.when(step == 0)
-    def _():
-        sums_of[...] = jnp.zeros_like(sums_of)
-        value = lax.rsqrt(total[...] / count + 1e-06)
-        for p in range(4):
-            scale[pl.ds(p, depth, stride=4), :] = value
-
+    slots, piece = staged.shape[:2]
+    unroll = piece // depth
     wide = 4 * depth
+    value = lax.rsqrt(total[...] / count + 1e-06)
+    for p in range(4):
+        scale[pl.ds(p, depth, stride=4), :] = value
     lane = lax.broadcasted_iota(jnp.int32, (wide, LANES), 1)
 
-    first = step * (readings // depth)
+    def out(g):
+        to = jacobian.at[pl.ds(pl.multiple_of(g * piece, piece), piece)]
+        return pltpu.make_async_copy(staged.at[g % slots], to, out_sem.at[g % slots])
 
     def some(g, sums):
+        @pl.when(g >= slots)
+        def _():
+            out(g - slots).wait()
+
         columns = [
-            jnp.sum(jnp.where(lane == first + UNROLL * g + u, scale[...], 0.0), axis=-1, keepdims=True)
-            for u in range(UNROLL)
+            jnp.sum(jnp.where(lane == unroll * g + u, scale[...], 0.0), axis=-1, keepdims=True)
+            for u in range(unroll)
         ]
-        for u in range(UNROLL):
-            i = UNROLL * g + u
-            rows = pl.ds(pl.multiple_of((first + i) * wide, wide), wide)
-            put = pl.ds(pl.multiple_of(i * depth, depth), depth)
+        for u in range(unroll):
+            rows = pl.ds(pl.multiple_of((unroll * g + u) * wide, wide), wide)
             for c in range(cells // LANES):
                 normed = sens[c, rows, :] * columns[u]
-                jacobian[put, :, pl.ds(c * LANES, LANES)] = normed.reshape(depth, 4, LANES).astype(jnp.bfloat16)
+                staged[g % slots, pl.ds(u * depth, depth), :, pl.ds(c * LANES, LANES)] = normed.reshape(
+                    depth, 4, LANES
+                ).astype(jnp.bfloat16)
                 square = jnp.sum((normed * normed).reshape(wide // 8, 8, LANES), axis=0)
                 sums = sums[:c] + (sums[c] + square,) + sums[c + 1:]
+        part = piece // PARTS
+        for h in range(PARTS):
+            pltpu.make_async_copy(
+                staged.at[g % slots, pl.ds(h * part, part)],
+                jacobian.at[pl.ds(pl.multiple_of(g * piece + h * part, part), part)],
+                out_sem.at[g % slots],
+            ).start()
         return sums
 
-    sums = lax.fori_loop(
-        0, readings // depth // UNROLL, some,
-        tuple(sums_of[c] for c in range(cells // LANES)),
-    )
-    for c, total_of in enumerate(sums):
-        sums_of[c] = total_of
-
-    @pl.when(step == pl.num_programs(0) - 1)
-    def _():
-        for c in range(cells // LANES):
-            coverage[pl.ds(c, 1), :] = jnp.sum(sums_of[c], axis=0, keepdims=True)
+    pieces = readings // piece
+    sums = lax.fori_loop(0, pieces, some, (jnp.zeros((8, LANES), jnp.float32),) * (cells // LANES))
+    for c, sum_of in enumerate(sums):
+        coverage[pl.ds(c, 1), :] = jnp.sum(sum_of, axis=0, keepdims=True)
+
+    @pl.loop(max(pieces - slots, 0), pieces)
+    def _(g):
+        out(g).wait()
 
 
 def normalise(sens, total, count):
     chunks, rows, _ = sens.shape
     readings, cells = rows // 4, chunks * LANES
-    block = 512
+    piece = UNROLL * total.shape[0]
+    slots = min(SLOTS, readings // piece)
+    in_vmem = pl.BlockSpec(memory_space=pltpu.VMEM)
     return pl.pallas_call(
         functools.partial(norm_kernel, count),
-        grid=(readings // block,),
-        in_specs=[
-            pl.BlockSpec(memory_space=pltpu.VMEM),
-            pl.BlockSpec(memory_space=pltpu.VMEM),
-        ],
-        out_specs=[
-            pl.BlockSpec((block, 4, cells), lambda i: (i, 0, 0)),
-            pl.BlockSpec((chunks, LANES), lambda i: (0, 0)),
-        ],
+        in_specs=[in_vmem, in_vmem],
+        out_specs=[pl.BlockSpec(memory_space=pl.ANY), in_vmem],
         out_shape=[
             jax.ShapeDtypeStruct((readings, 4, cells), jnp.bfloat16),
             jax.ShapeDtypeStruct((chunks, LANES), jnp.float32),
         ],
         scratch_shapes=[
             pltpu.VMEM((4 * total.shape[0], LANES), jnp.float32),
-            pltpu.VMEM((chunks, 8, LANES), jnp.float32),
+            pltpu.VMEM((slots, piece, 4, cells), jnp.bfloat16),
+            pltpu.SemaphoreType.DMA((slots,)),
         ],
         compiler_params=pltpu.CompilerParams(vmem_limit_bytes=8 * 2**20),
         name="norm",

time: 297 us -> 296 us (level)
  no operation moved by 1% of the time
where the time goes in v3:
time: 296 us
  Pallas kernels  295 us (100%)
    pallas_call x1, Pallas kernels, sensitivities(): pl.pallas_call(functools.partial(exchange_kernel, n), out_shape=[pltpu.VM...  289 us

profile of v3, /device:TPU:0, one launch (start us, length us, event | category | flops | bytes accessed | tf_op | source)
XLA Modules:
  0.0 295.5 jit_solution(5977009170602209161)
XLA Ops:
  0.6 289.1 %exchange.1 = (f32[4,8192,128]{2,1,0:T(8,128)S(1)}, f32[16,128]{1,0:T(8,128)S(1)}) custom-call(s32[4,2048]{1,0:T(4,128)} %bitcast.8, bf16[3,256,8192]{2,1,0:T(8,128)(2,1)} %bitcast.7, f32[4,128]{1,0:T(4,128)} %bitcast.9, f32[4,128]{1,0:T(4,128)} %bitcast.10, f32[4,128]{1,0:T(4,128)} %bitcast.11, f32[4,128]{1,0:T(4,128)} %bitcast.12), custom_call_target="tpu_custom_call" | custom-call | tf_op jit(solution)/shard_map/exchange/pallas_call | solution.py:274
  289.7 5.8 %norm.1 = (bf16[2048,4,512]{2,1,0:T(4,128)(2,1)}, f32[4,128]{1,0:T(4,128)}) custom-call(f32[4,8192,128]{2,1,0:T(8,128)S(1)} %get-tuple-element.6.sens, f32[16,128]{1,0:T(8,128)S(1)} %get-tuple-element.7.total), custom_call_target="tpu_custom_call" | custom-call | tf_op jit(solution)/shard_map/norm/pallas_call | solution.py:364

commit v4 on v3

--- a/solution.py
+++ b/solution.py
@@ -13,7 +13,7 @@
 PARTS = 8
 SLOTS = 4
 UNROLL = 16
-TILE = 1024
+TILE = 2048
 
 
 def greet(n, me):

time: 296 us -> 296 us (level)
  no operation moved by 1% of the time
where the time goes in v4:
time: 296 us; the launch traced here: 295 us
  Pallas kernels  295 us (100%)
    pallas_call x1, Pallas kernels, sensitivities(): pl.pallas_call(functools.partial(exchange_kernel, n), out_shape=[pltpu.VM...  289 us

profile of v4, /device:TPU:0, one launch (start us, length us, event | category | flops | bytes accessed | tf_op | source)
XLA Modules:
  0.0 295.4 jit_solution(17276040886871472627)
XLA Ops:
  0.6 288.9 %exchange.1 = (f32[4,8192,128]{2,1,0:T(8,128)S(1)}, f32[16,128]{1,0:T(8,128)S(1)}) custom-call(s32[4,2048]{1,0:T(4,128)} %bitcast.8, bf16[3,256,8192]{2,1,0:T(8,128)(2,1)} %bitcast.7, f32[4,128]{1,0:T(4,128)} %bitcast.9, f32[4,128]{1,0:T(4,128)} %bitcast.10, f32[4,128]{1,0:T(4,128)} %bitcast.11, f32[4,128]{1,0:T(4,128)} %bitcast.12), custom_call_target="tpu_custom_call" | custom-call | tf_op jit(solution)/shard_map/exchange/pallas_call | solution.py:274
  289.6 5.8 %norm.1 = (bf16[2048,4,512]{2,1,0:T(4,128)(2,1)}, f32[4,128]{1,0:T(4,128)}) custom-call(f32[4,8192,128]{2,1,0:T(8,128)S(1)} %get-tuple-element.6.sens, f32[16,128]{1,0:T(8,128)S(1)} %get-tuple-element.7.total), custom_call_target="tpu_custom_call" | custom-call | tf_op jit(solution)/shard_map/norm/pallas_call | solution.py:364
